TPU v7x, 32 devices: a whole 2x2x4 slice. The times are simulated.
32 devices in a mesh: seq: 8 (over z, core), rep: 4 (over y, x).
Axes of the slice: x: 2, y: 2, z: 4, core: 2. Of those that a mesh axis runs over, the one named last changes fastest.
Arguments:
- lengths: int32 [4], P('rep'), may hold values from 384 to 3072
- prompt_query: bfloat16 [4, 3072, 4096], P('rep', 'seq'), may hold values from -6 to 6
- prompt_key: bfloat16 [4, 3072, 4096], P('rep', 'seq'), may hold values from -0.52734375 to 0.52734375
- prompt_value: bfloat16 [4, 3072, 4096], P('rep', 'seq'), may hold values from -6 to 6
- prompt_decay: float32 [4, 32, 3072], P('rep', None, 'seq'), may hold values from -1 to 0
- step_query: bfloat16 [4, 4, 4096], P(None, 'rep', 'seq'), may hold values from -6 to 6
- step_key: bfloat16 [4, 4, 4096], P(None, 'rep', 'seq'), may hold values from -6 to 6
- step_value: bfloat16 [4, 4, 4096], P(None, 'rep', 'seq'), may hold values from -6 to 6
- step_decay: float32 [4, 4, 32], P(None, 'rep', 'seq'), may hold values from -1 to 0
- out_weight: bfloat16 [4096, 6144], P('seq', 'rep'), may hold values from -0.09375 to 0.09375
Outputs:
- prompt_out: bfloat16 [4, 3072, 4096], P('rep', 'seq')
- step_out: bfloat16 [4, 4, 6144], P(None, None, 'rep')
All inputs are finite; a program needn't handle non-finite values.
Results may differ from a plain program's by a relative error of at most 0.0029.
The roundings to bfloat16 on the way count: a program that leaves them out, or rounds other values in their place, can miss the bound.
Values may be sent and summed in bfloat16 or wider, within the bound.
A program may use at most 128 MiB of HBM per device.

v0:
```python
import jax
import jax.numpy as jnp
from jax import lax
from jax.sharding import PartitionSpec as P

HEAD_DIM = 128


epsilon = 1e-06


def entering(array, axis, combine, identity, reverse):
    devices, position = (lax.axis_size(axis), lax.axis_index(axis))
    everything = jax.tree.map(lambda part: lax.all_gather(part, axis), array)
    start = jax.tree.map(
        lambda part, zero: jnp.broadcast_to(jnp.asarray(zero, part.dtype), part.shape),
        array,
        identity,
    )

    def hop(k, before):
        at = devices - 1 - k if reverse else k
        reached = at > position if reverse else at < position
        new = combine(before, jax.tree.map(lambda part: part[at], everything))
        return jax.tree.map(lambda a, b: jnp.where(reached, a, b), new, before)

    return lax.fori_loop(0, devices, hop, start)


def combine_pair(earlier, later_part):
    return (
        earlier[0] * jnp.exp(later_part[1])[:, :, None, None] + later_part[0],
        earlier[1] + later_part[1],
    )


def add_sums(first, latter_portion):
    return first + latter_portion


def shards(
    lengths,
    prompt_query,
    prompt_key,
    prompt_value,
    prompt_decay,
    step_query,
    step_key,
    step_value,
    step_decay,
    out_weight,
):
    req_local, block_len, feat_width = prompt_query.shape
    heads_all = feat_width // HEAD_DIM
    seq_index = lax.axis_index("seq")
    position = seq_index * block_len + jnp.arange(block_len, dtype=jnp.int32)
    live_mask = (position[None, :] < lengths[:, None]).astype(jnp.float32)
    shaped = (req_local, block_len, heads_all, HEAD_DIM)
    query_rows = prompt_query.reshape(shaped)
    keys_live = prompt_key.reshape(shaped) * live_mask[:, :, None, None].astype(jnp.bfloat16)
    value_input_rows = prompt_value.reshape(shaped)
    log_decay = prompt_decay * live_mask[:, None, :]
    cumulative = jnp.cumsum(log_decay, axis=2)
    block_decay = cumulative[:, :, -1]
    scores = jnp.einsum(
        "rthd,rshd->rhts", query_rows, keys_live, preferred_element_type=jnp.float32
    )
    offsets = jnp.arange(block_len, dtype=jnp.int32)
    causal = (offsets[:, None] >= offsets[None, :])[None, None]
    log_gaps = cumulative[:, :, :, None] - cumulative[:, :, None, :]
    decay_mask = jnp.where(causal, jnp.exp(jnp.where(causal, log_gaps, 0.0)), 0.0)
    weighted = (scores * decay_mask).astype(jnp.bfloat16)
    within = jnp.einsum(
        "rhts,rshd->rthd", weighted, value_input_rows, preferred_element_type=jnp.float32
    )
    key_scaled_rows = (
        keys_live.astype(jnp.float32)
        * jnp.exp(block_decay[:, None, :] - cumulative.transpose(0, 2, 1))[:, :, :, None]
    ).astype(jnp.bfloat16)
    block_local_state = jnp.einsum(
        "rthk,rthv->rhkv", key_scaled_rows, value_input_rows, preferred_element_type=jnp.float32
    )
    carry_in, _ = entering(
        (block_local_state, block_decay),
        "seq",
        combine_pair,
        (jnp.zeros_like(block_local_state), jnp.zeros_like(block_decay)),
        False,
    )
    lower_carry_state = carry_in.astype(jnp.bfloat16)
    carried_state_term = jnp.einsum(
        "rthk,rhkv->rthv", query_rows, lower_carry_state, preferred_element_type=jnp.float32
    )
    carried_state_term = carried_state_term * jnp.exp(cumulative).transpose(0, 2, 1)[:, :, :, None]
    attended = (within + carried_state_term).reshape(req_local, block_len, feat_width)
    prompt_out = (
        attended
        * lax.rsqrt(jnp.mean(attended * attended, axis=-1, keepdims=True) + epsilon)
        * live_mask[:, :, None]
    ).astype(jnp.bfloat16)
    head_share = heads_all // lax.axis_size("seq")
    later_decay = entering(block_decay, "seq", add_sums, jnp.zeros_like(block_decay), True)
    decode_state = lax.psum_scatter(
        block_local_state * jnp.exp(later_decay)[:, :, None, None],
        "seq",
        scatter_dimension=1,
        tiled=True,
    )
    steps_count, reqs_here, part_width = step_query.shape
    step_shape = (steps_count, reqs_here, head_share, HEAD_DIM)
    step_q = step_query.reshape(step_shape)
    step_k = step_key.reshape(step_shape)
    step_v = step_value.reshape(step_shape)
    heard_list = []
    for step_num in range(steps_count):
        outer_term = (
            step_k[step_num].astype(jnp.float32)[:, :, :, None]
            * step_v[step_num].astype(jnp.float32)[:, :, None, :]
        )
        decode_state = decode_state * jnp.exp(step_decay[step_num])[:, :, None, None] + outer_term
        heard_list.append(
            jnp.einsum(
                "rhk,rhkv->rhv",
                step_q[step_num].astype(jnp.float32),
                decode_state,
                precision=lax.Precision.HIGHEST,
            )
        )
    step_heads = jnp.stack(heard_list).reshape(steps_count, reqs_here, part_width)
    sum_squares = lax.psum(jnp.sum(step_heads * step_heads, axis=-1), "seq")
    normed = (step_heads * lax.rsqrt(sum_squares[:, :, None] / feat_width + epsilon)).astype(
        jnp.bfloat16
    )
    projected = jnp.einsum(
        "srf,fc->src",
        lax.all_gather(normed, "rep", axis=1, tiled=True),
        out_weight,
        preferred_element_type=jnp.float32,
    )
    step_out = lax.psum(projected, "seq").astype(jnp.bfloat16)
    return (prompt_out, step_out)


def solution(mesh):
    return jax.shard_map(
        shards,
        mesh=mesh,
        in_specs=(
            P("rep"),
            P("rep", "seq", None),
            P("rep", "seq", None),
            P("rep", "seq", None),
            P("rep", None, "seq"),
            P(None, "rep", "seq"),
            P(None, "rep", "seq"),
            P(None, "rep", "seq"),
            P(None, "rep", "seq"),
            P("seq", "rep"),
        ),
        out_specs=(P("rep", "seq", None), P(None, None, "rep")),
        check_vma=False,
    )
```

profile of v0, /device:TPU:0, one launch (start us, length us, event | category | flops | bytes accessed | tf_op | source)
XLA Modules:
  0.0 291.2 jit_solution(8037963356052265298)
XLA Ops:
  7.2 0.0 copy-start
  7.2 0.0 reduce-scatter.2.cloned.1.call-start
  8.0 0.8 copy_bitcast_fusion
  8.8 0.9 reduce-window.6
  9.7 0.2 slice_reduce_fusion
  9.9 0.1 copy.82
  10.0 0.1 broadcast.233
  10.1 0.2 slice_reduce_fusion.1
  10.3 0.1 exponential_bitcast_fusion.2
  10.4 4.7 %copy.81 = bf16[1,384,4096]{1,2,0:T(8,128)(2,1)} copy(bf16[1,384,4096]{2,1,0:T(8,128)(2,1)} %param.16) | data formatting | bytes 6291456 | tf_op jit(solution)/shard_map/reshape | solution.py:60
  15.1 4.4 %copy.85 = bf16[48,8,32,128]{3,2,1,0:T(8,128)(2,1)} copy(bf16[48,8,32,128]{3,1,2,0:T(8,128)(2,1)} %bitcast.157) | data formatting | bytes 6291456
  19.5 0.1 copy.61
  19.6 13.4 %all-gather = f32[8,32,1]{1,2,0:T(1,128)S(1)} all-gather(f32[1,32,1]{1,2,0:T(1,128)S(1)} %copy.61), channel_id=2, replica_groups=mesh['seq'=8,'rep'=4] {'seq'}, dimensions={0}, use_global_device_ids=true | all-gather | bytes 1152 | tf_op jit(solution)/shard_map/all_gather | solution.py:14
  32.9 0.3 while.31
  33.2 7.5 %fusion.11 = f32[32,128,128]{2,1,0:T(8,128)} fusion(f32[384,32]{0,1:T(8,128)S(1)} %exponential_bitcast_fusion.2, bf16[384,32,128]{2,1,0:T(8,128)(2,1)} %bitcast.161, bf16[384,32,128]{0,2,1:T(8,128)(2,1)} %bitcast.159, bf16[384]{0:T(512)(128)(2,1)S(1)} %get-tuple-element.310), kind=kOutput, calls=%fused_computation.18 | convolution fusion | flops 408944640 | bytes 8438528 | tf_op jit(solution)/shard_map/rthk,rthv->rhkv/dot_general | solution.py:80
  40.7 3.1 %multiply_bitcast_fusion = f32[1,32,128,128]{3,2,1,0:T(8,128)} fusion(f32[32,128,128]{2,1,0:T(8,128)} %fusion.11, f32[32]{0:T(128)S(1)} %exponential_bitcast_fusion.7), kind=kLoop, calls=%fused_computation.27 | loop fusion | flops 524288 | bytes 4194432 | tf_op jit(solution)/shard_map/mul | solution.py:104
  43.8 0.0 reduce-scatter.2.cloned.1.call-update
  43.9 0.2 all-gather.4.cloned.1.call-start
  44.1 0.5 all-gather.4.cloned.1.call-update
  44.7 0.0 copy-start.4
  44.7 0.0 copy-start.1
  44.7 0.0 copy-start.2
  44.7 4.4 %copy.86 = bf16[48,8,32,128]{3,2,1,0:T(8,128)(2,1)} copy(bf16[48,8,32,128]{3,1,2,0:T(8,128)(2,1)} %bitcast.158) | data formatting | bytes 6291456
  49.3 14.2 %fusion.2 = f32[32,384,128]{1,2,0:T(8,128)} fusion(f32[32,384]{1,0:T(8,128)S(1)} %bitcast_add_fusion.1, pred[384,384]{0,1:T(8,128)(4,1)S(1)} %iota_compare_fusion, bf16[384,32,128]{2,1,0:T(8,128)(2,1)} %bitcast.162, bf16[384,32,128]{2,1,0:T(8,128)(2,1)} %bitcast.154, bf16[384,32,128]{0,2,1:T(8,128)(2,1)} %bitcast.160, bf16[384]{0:T(512)(128)(2,1)S(1)} %get-tuple-element.310), kind=kOutput, calls=%fused_computation.7 | convolution fusion | flops 2441084928 | bytes 15926016 | tf_op jit(solution)/shard_map/rhts,rshd->rthd/dot_general | solution.py:73
  63.5 14.5 %reduce-scatter.2.cloned.1.call-done = f32[1,4,128,128]{3,2,1,0:T(8,128)} async-done(((f32[1,32,128,128]{3,2,1,0:T(8,128)}), f32[1,4,128,128]{3,2,1,0:T(8,128)}) %reduce-scatter.2.cloned.1.call-update) | async-done | bytes 262160 | tf_op jit(solution)/shard_map/reduce_scatter | solution.py:103
  78.0 1.3 convolution_bitcast_fusion.3
  79.3 1.4 convolution_bitcast_fusion.2
  80.6 1.4 convolution_bitcast_fusion.1
  82.1 1.5 convolution_bitcast_fusion
  83.6 0.1 multiply_reduce_fusion.1
  83.7 15.0 %psum.14 = f32[4,1]{0,1:T(1,128)S(1)} all-reduce(f32[4,1]{0,1:T(1,128)S(1)} %bitcast.187), channel_id=1, replica_groups=mesh['seq'=8,'rep'=4] {'seq'}, use_global_device_ids=true, to_apply=%region_9.10 | all-reduce | flops 4 | bytes 32 | tf_op jit(solution)/shard_map/psum | solution.py:130
  98.7 0.1 multiply_convert_fusion.3
  98.7 8.2 %all_gather.16 = bf16[4,4,512]{2,0,1:T(4,128)(2,1)S(1)} all-gather(bf16[4,1,512]{2,0,1:T(4,128)(2,1)S(1)} %multiply_convert_fusion.3), channel_id=1, replica_groups=mesh['seq'=8,'rep'=4] {'rep'}, dimensions={1}, use_global_device_ids=true | all-gather | bytes 20480 | tf_op jit(solution)/shard_map/all_gather | solution.py:136
  106.9 0.3 fusion.24
  107.2 30.3 %psum.15 = bf16[4,4,1536]{2,1,0:T(4,128)(2,1)} all-reduce(f32[4,4,1536]{2,1,0:T(4,128)S(1)} %fusion.24), channel_id=1, replica_groups=mesh['seq'=8,'rep'=4] {'seq'}, use_global_device_ids=true, to_apply=%region_10.11 | all-reduce | flops 24576 | bytes 147456 | tf_op jit(solution)/shard_map/psum | solution.py:140
  137.5 93.6 %all-gather.4.cloned.1.call-done = f32[256,128,128]{2,1,0:T(8,128)} async-done(((f32[32,128,128]{2,1,0:T(8,128)}), f32[256,128,128]{2,1,0:T(8,128)}) %all-gather.4.cloned.1.call-update) | async-done | bytes 16777232 | tf_op jit(solution)/shard_map/all_gather | solution.py:14
  231.1 30.4 %while.30 = (s32[]{:T(128)}, f32[1,32,128,128]{3,2,1,0:T(8,128)}, s32[]{:T(128)}, f32[8,1,32]{2,1,0:T(1,128)S(1)}, f32[8,1,32,128,128]{4,3,2,1,0:T(8,128)}, /*index=5*/s32[]{:T(128)}, s32[]{:T(128)}) while((s32[]{:T(128)}, f32[1,32,128,128]{3,2,1,0:T(8,128)}, s32[]{:T(128)}, f32[8,1,32]{2,1,0:T(1,128)S(1)}, ...), condition=%wide.region_3.4_spmd.clone, body=%wide.region_2.3_spmd.clone.sunk | while | flops 2097156 | bytes 6291945 | solution.py:27
  231.1 3.2 %fusion.66 = f32[1,32,128,128]{3,2,1,0:T(8,128)} fusion(f32[8,1,32,128,128]{4,3,2,1,0:T(8,128)} %get-tuple-element.385, s32[]{:T(128)} %get-tuple-element.374, f32[1,32,128,128]{3,2,1,0:T(8,128)} %get-tuple-element.375, f32[32]{0:T(128)S(1)} %exponential_bitcast_fusion.9, pred[]{:T(512)S(6)} %compare.6, pred[]{:T(512)S(6)} %lt.79), kind=kLoop, calls=%fused_computation.1.clone.1 | loop fusion | flops 2097152 | bytes 6291590 | tf_op jit(solution)/shard_map/while/body/eval_jaxpr/jit(_where)/select_n | solution.py:25
  234.4 3.9 %fusion.66 = f32[1,32,128,128]{3,2,1,0:T(8,128)} fusion(f32[8,1,32,128,128]{4,3,2,1,0:T(8,128)} %get-tuple-element.385, s32[]{:T(128)} %get-tuple-element.374, f32[1,32,128,128]{3,2,1,0:T(8,128)} %get-tuple-element.375, f32[32]{0:T(128)S(1)} %exponential_bitcast_fusion.9, pred[]{:T(512)S(6)} %compare.6, pred[]{:T(512)S(6)} %lt.79), kind=kLoop, calls=%fused_computation.1.clone.1 | loop fusion | flops 2097152 | bytes 6291590 | tf_op jit(solution)/shard_map/while/body/eval_jaxpr/jit(_where)/select_n | solution.py:25
  238.2 3.9 %fusion.66 = f32[1,32,128,128]{3,2,1,0:T(8,128)} fusion(f32[8,1,32,128,128]{4,3,2,1,0:T(8,128)} %get-tuple-element.385, s32[]{:T(128)} %get-tuple-element.374, f32[1,32,128,128]{3,2,1,0:T(8,128)} %get-tuple-element.375, f32[32]{0:T(128)S(1)} %exponential_bitcast_fusion.9, pred[]{:T(512)S(6)} %compare.6, pred[]{:T(512)S(6)} %lt.79), kind=kLoop, calls=%fused_computation.1.clone.1 | loop fusion | flops 2097152 | bytes 6291590 | tf_op jit(solution)/shard_map/while/body/eval_jaxpr/jit(_where)/select_n | solution.py:25
  242.1 3.9 %fusion.66 = f32[1,32,128,128]{3,2,1,0:T(8,128)} fusion(f32[8,1,32,128,128]{4,3,2,1,0:T(8,128)} %get-tuple-element.385, s32[]{:T(128)} %get-tuple-element.374, f32[1,32,128,128]{3,2,1,0:T(8,128)} %get-tuple-element.375, f32[32]{0:T(128)S(1)} %exponential_bitcast_fusion.9, pred[]{:T(512)S(6)} %compare.6, pred[]{:T(512)S(6)} %lt.79), kind=kLoop, calls=%fused_computation.1.clone.1 | loop fusion | flops 2097152 | bytes 6291590 | tf_op jit(solution)/shard_map/while/body/eval_jaxpr/jit(_where)/select_n | solution.py:25
  246.0 3.9 %fusion.66 = f32[1,32,128,128]{3,2,1,0:T(8,128)} fusion(f32[8,1,32,128,128]{4,3,2,1,0:T(8,128)} %get-tuple-element.385, s32[]{:T(128)} %get-tuple-element.374, f32[1,32,128,128]{3,2,1,0:T(8,128)} %get-tuple-element.375, f32[32]{0:T(128)S(1)} %exponential_bitcast_fusion.9, pred[]{:T(512)S(6)} %compare.6, pred[]{:T(512)S(6)} %lt.79), kind=kLoop, calls=%fused_computation.1.clone.1 | loop fusion | flops 2097152 | bytes 6291590 | tf_op jit(solution)/shard_map/while/body/eval_jaxpr/jit(_where)/select_n | solution.py:25
  249.9 3.9 %fusion.66 = f32[1,32,128,128]{3,2,1,0:T(8,128)} fusion(f32[8,1,32,128,128]{4,3,2,1,0:T(8,128)} %get-tuple-element.385, s32[]{:T(128)} %get-tuple-element.374, f32[1,32,128,128]{3,2,1,0:T(8,128)} %get-tuple-element.375, f32[32]{0:T(128)S(1)} %exponential_bitcast_fusion.9, pred[]{:T(512)S(6)} %compare.6, pred[]{:T(512)S(6)} %lt.79), kind=kLoop, calls=%fused_computation.1.clone.1 | loop fusion | flops 2097152 | bytes 6291590 | tf_op jit(solution)/shard_map/while/body/eval_jaxpr/jit(_where)/select_n | solution.py:25
  253.8 3.9 %fusion.66 = f32[1,32,128,128]{3,2,1,0:T(8,128)} fusion(f32[8,1,32,128,128]{4,3,2,1,0:T(8,128)} %get-tuple-element.385, s32[]{:T(128)} %get-tuple-element.374, f32[1,32,128,128]{3,2,1,0:T(8,128)} %get-tuple-element.375, f32[32]{0:T(128)S(1)} %exponential_bitcast_fusion.9, pred[]{:T(512)S(6)} %compare.6, pred[]{:T(512)S(6)} %lt.79), kind=kLoop, calls=%fused_computation.1.clone.1 | loop fusion | flops 2097152 | bytes 6291590 | tf_op jit(solution)/shard_map/while/body/eval_jaxpr/jit(_where)/select_n | solution.py:25
  257.6 3.9 %fusion.66 = f32[1,32,128,128]{3,2,1,0:T(8,128)} fusion(f32[8,1,32,128,128]{4,3,2,1,0:T(8,128)} %get-tuple-element.385, s32[]{:T(128)} %get-tuple-element.374, f32[1,32,128,128]{3,2,1,0:T(8,128)} %get-tuple-element.375, f32[32]{0:T(128)S(1)} %exponential_bitcast_fusion.9, pred[]{:T(512)S(6)} %compare.6, pred[]{:T(512)S(6)} %lt.79), kind=kLoop, calls=%fused_computation.1.clone.1 | loop fusion | flops 2097152 | bytes 6291590 | tf_op jit(solution)/shard_map/while/body/eval_jaxpr/jit(_where)/select_n | solution.py:25
  261.5 10.7 %multiply_reduce_fusion = (f32[384]{0:T(512)S(1)}, f32[1,384,32,128]{1,3,2,0:T(8,128)}) fusion(f32[384,32]{0,1:T(8,128)S(1)} %get-tuple-element.291, bf16[384,32,128]{2,1,0:T(8,128)(2,1)} %bitcast.155, f32[1,32,128,128]{3,2,1,0:T(8,128)} %get-tuple-element.206, f32[32,384,128]{1,2,0:T(8,128)} %fusion.2), kind=kOutput, calls=%fused_computation.15 | convolution fusion | flops 409468544 | bytes 17876480 | tf_op jit(solution)/shard_map/rthk,rhkv->rthv/dot_general | solution.py:91
  272.2 6.5 %copy.67 = f32[1,384,4096]{2,1,0:T(8,128)} copy(f32[1,384,4096]{1,2,0:T(8,128)} %bitcast.153) | data formatting | bytes 12582912 | tf_op jit(solution)/shard_map/reshape | solution.py:95
  278.8 5.6 %multiply_convert_fusion = bf16[1,384,4096]{2,1,0:T(8,128)(2,1)} fusion(f32[1,384,4096]{2,1,0:T(8,128)} %copy.67, f32[384]{0:T(512)S(1)} %get-tuple-element.309, f32[384]{0:T(512)S(1)} %add_rsqrt_fusion), kind=kLoop, calls=%fused_computation.14 | loop fusion | flops 4718592 | bytes 9440256 | tf_op jit(solution)/shard_map/convert_element_type | solution.py:100
  (39 shorter events, 0.4 us)
Async XLA Ops:
  7.2 99.7 %copy-start = (bf16[512,1536]{1,0:T(8,128)(2,1)S(1)}, bf16[512,1536]{1,0:T(8,128)(2,1)}, u32[]{:S(2)}) copy-start(bf16[512,1536]{1,0:T(8,128)(2,1)} %param.23) | copy-start | bytes 4718596
  7.2 70.8 %reduce-scatter.2.cloned.1.call-start = ((), (), s32[]{:S(2)}) async-start(), calls=%async_computation.1 | async-start | bytes 2359296 | tf_op jit(solution)/shard_map/reduce_scatter | solution.py:103
  43.9 187.3 %all-gather.4.cloned.1.call-start = ((), (), s32[]{:S(2)}) async-start(), calls=%async_computation.2 | async-start | bytes 18874368 | tf_op jit(solution)/shard_map/all_gather | solution.py:14
  44.7 4.5 %copy-start.4 = (f32[4,1,4]{2,1,0:T(1,128)S(1)}, f32[4,1,4]{2,1,0:T(1,128)}, u32[]{:S(2)}) copy-start(f32[4,1,4]{2,1,0:T(1,128)} %param.22) | copy-start | bytes 196
  44.7 4.5 %copy-start.1 = (bf16[4,1,512]{2,0,1:T(4,128)(2,1)S(1)}, bf16[4,1,512]{2,0,1:T(4,128)(2,1)}, u32[]{:S(2)}) copy-start(bf16[4,1,512]{2,0,1:T(4,128)(2,1)} %param.20) | copy-start | bytes 12292
  44.7 4.5 %copy-start.2 = (bf16[4,1,512]{2,0,1:T(4,128)(2,1)S(1)}, bf16[4,1,512]{2,0,1:T(4,128)(2,1)}, u32[]{:S(2)}) copy-start(bf16[4,1,512]{2,0,1:T(4,128)(2,1)} %param.21) | copy-start | bytes 12292
  49.3 28.8 %copy-start.3 = (bf16[4,1,512]{2,0,1:T(4,128)(2,1)S(1)}, bf16[4,1,512]{2,0,1:T(4,128)(2,1)}, u32[]{:S(2)}) copy-start(bf16[4,1,512]{2,0,1:T(4,128)(2,1)} %param.19) | copy-start | bytes 12292
Sparse Core Ops, SparseCore 0:
  44.0 33.9 reduce-scatter.1
  79.6 151.4 all-gather.3
where the time goes:
time: 292 us; the launch traced here: 291 us
  waiting for transfers between devices  109 us (37%)
  blocking collectives  66.8 us (23%)
  other arithmetic  41.3 us (14%)
  matrix products  38.3 us (13%)
  local copies, waits for them, and re-layouts  20.8 us (7%)
  between operations  15 us (5%)
    all_gather x1, waiting for transfers between devices, entering(): everything = jax.tree.map(lambda part: lax.all_gather(part, axis), array)  93.6 us
    select_n x16, other arithmetic, hop(): return jax.tree.map(lambda a, b: jnp.where(reached, a, b), new, before)  30.5 us
    psum x1, blocking collectives, shards(): step_out = lax.psum(projected, 'seq').astype(jnp.bfloat16)  30.3 us
    psum x1, blocking collectives, shards(): sum_squares = lax.psum(jnp.sum(step_heads * step_heads, axis=-1), 'seq')  15 us
    reduce_scatter x1, waiting for transfers between devices, shards(): lax.psum_scatter(block_local_state * jnp.exp(later_decay)[:, :, None, Non...  14.5 us
    dot_general x1, matrix products, shards(): jnp.einsum('rhts,rshd->rthd', weighted, value_input_rows, preferred_eleme...  14.2 us
    all_gather x1, blocking collectives, entering(): everything = jax.tree.map(lambda part: lax.all_gather(part, axis), array)  13.4 us
    dot_general x1, matrix products, shards(): jnp.einsum('rthk,rhkv->rthv', query_rows, lower_carry_state, preferred_el...  10.7 us
  transfers between devices with their start and end apart: 2, of which 2 were waited for; matrix products, arithmetic and copies ran while one was open for 9% of the time, Pallas kernels for 0%

commit v1 on v0

v1 whole, which is shorter than its diff:
```python
import functools
import jax
import jax.numpy as jnp
from jax import lax
from jax.experimental import pallas as pl
from jax.experimental.pallas import tpu as pltpu
from jax.sharding import PartitionSpec as P

HEAD_DIM = 128
CHUNK = 2
epsilon = 1e-06
MESH = pl.DeviceIdType.MESH
F32 = jnp.float32
BF16 = jnp.bfloat16


def dot(a, b, ca, cb, precision=None):
    return lax.dot_general(
        a, b, (((ca,), (cb,)), ((), ())), preferred_element_type=F32, precision=precision
    )


def prompt_kernel(
    n, heads, block,
    len_ref, q_ref, k_ref, v_ref, d_ref,
    out_ref, fin_ref,
    cum_b, cum_row, total, state, inbox, attended, squares, live_b,
    send_sem, recv_sem, fin_send, fin_recv,
):
    me = lax.axis_index("seq")
    rep = lax.axis_index("rep")
    last = n - 1
    share = heads // n
    chunk = min(CHUNK, share)
    chunks = heads // chunk
    per_owner = share // chunk

    barrier = pltpu.get_barrier_semaphore()
    for step in range(1, n):
        pl.semaphore_signal(
            barrier, inc=1, device_id=(lax.rem(me + step, n), rep), device_id_type=MESH
        )

    length = len_ref[0]
    start = me * block
    row_live = (lax.broadcasted_iota(jnp.int32, (1, block), 1) + start < length).astype(F32)
    live_b[...] = (
        lax.broadcasted_iota(jnp.int32, (block, HEAD_DIM), 0) + start < length
    ).astype(F32)
    log_decay = d_ref[0] * row_live
    below = (
        lax.broadcasted_iota(jnp.int32, (block, block), 0)
        >= lax.broadcasted_iota(jnp.int32, (block, block), 1)
    ).astype(F32)
    cum = dot(log_decay, below, 1, 1, lax.Precision.HIGHEST)
    for h in range(heads):
        cum_row[h] = cum[h : h + 1, :]
    cum_t = dot(below, log_decay, 1, 1, lax.Precision.HIGHEST)
    for h in range(heads):
        cum_b[h] = jnp.broadcast_to(cum_t[:, h : h + 1], (block, HEAD_DIM))
        total[h] = cum_b[h, block - 1 :, :]

    def columns(h):
        return pl.ds(pl.multiple_of(h * HEAD_DIM, HEAD_DIM), HEAD_DIM)

    def to_right(c):
        part = pl.ds(c * chunk, chunk)
        return pltpu.make_async_remote_copy(
            src_ref=state.at[part],
            dst_ref=inbox.at[part],
            send_sem=send_sem.at[c],
            recv_sem=recv_sem.at[c],
            device_id=(lax.rem(me + 1, n), rep),
            device_id_type=MESH,
        )

    def to_owner(c, owner):
        return pltpu.make_async_remote_copy(
            src_ref=state.at[pl.ds(c * chunk, chunk)],
            dst_ref=fin_ref.at[pl.ds((c % per_owner) * chunk, chunk)],
            send_sem=fin_send.at[c],
            recv_sem=fin_recv.at[c % per_owner],
            device_id=(owner, rep),
            device_id_type=MESH,
        )

    pl.semaphore_wait(barrier, n - 1)

    @pl.loop(0, chunks)
    def _(c):
        for i in range(chunk):
            h = c * chunk + i
            keys = k_ref[0, :, columns(h)].astype(F32) * live_b[...]
            scaled = (keys * jnp.exp(total[h] - cum_b[h])).astype(BF16)
            state[h] = dot(scaled, v_ref[0, :, columns(h)], 0, 0)

        @pl.when(me == 0)
        def _():
            to_right(c).start()

    tile = HEAD_DIM
    tiles = block // tile
    causal = (
        lax.broadcasted_iota(jnp.int32, (tile, tile), 0)
        >= lax.broadcasted_iota(jnp.int32, (tile, tile), 1)
    )
    squares[...] = jnp.zeros_like(squares)

    @pl.when(me == 0)
    def _():
        inbox[...] = jnp.zeros_like(inbox)

    @pl.loop(0, chunks)
    def _(c):
        @pl.when(me > 0)
        def _():
            to_right(c).wait_recv()
            for i in range(chunk):
                h = c * chunk + i
                state[h] = inbox[h] * jnp.exp(total[h]) + state[h]

            @pl.when(me < last)
            def _():
                to_right(c).start()

            @pl.when(me == last)
            def _():
                owner = c // per_owner

                @pl.when(owner != last)
                def _():
                    to_owner(c, owner).start()

                @pl.when(owner == last)
                def _():
                    fin_ref[pl.ds((c % per_owner) * chunk, chunk)] = state[
                        pl.ds(c * chunk, chunk)
                    ]

        for i in range(chunk):
            h = c * chunk + i
            query = q_ref[0, :, columns(h)]
            keys = (k_ref[0, :, columns(h)].astype(F32) * live_b[...]).astype(BF16)
            values = v_ref[0, :, columns(h)]
            carried = jnp.exp(cum_b[h]) * dot(query, inbox[h].astype(BF16), 1, 0)
            for t in range(tiles):
                rows = slice(t * tile, (t + 1) * tile)
                width = (t + 1) * tile
                scores = dot(query[rows], keys[:width], 1, 1)
                pieces = []
                for s in range(t + 1):
                    cols = slice(s * tile, (s + 1) * tile)
                    gap = cum_b[h, rows, :] - cum_row[h, :, cols]
                    if s == t:
                        decay = jnp.where(causal, jnp.exp(jnp.where(causal, gap, 0.0)), 0.0)
                    else:
                        decay = jnp.exp(gap)
                    pieces.append((scores[:, cols] * decay).astype(BF16))
                mixed = pieces[0] if t == 0 else jnp.concatenate(pieces, axis=1)
                both = dot(mixed, values[:width], 1, 0) + carried[rows]
                attended[rows, columns(h)] = both
                squares[rows, :] += both * both

    for t in range(tiles):
        rows = slice(t * tile, (t + 1) * tile)
        mean = jnp.sum(squares[rows, :], axis=1, keepdims=True) / (heads * HEAD_DIM)
        scale = jnp.broadcast_to(lax.rsqrt(mean + epsilon), (tile, HEAD_DIM)) * live_b[rows, :]
        squares[rows, :] = scale

    @pl.loop(0, heads)
    def _(h):
        out_ref[0, :, columns(h)] = (attended[:, columns(h)] * squares[...]).astype(BF16)

    @pl.when(me < last)
    def _():
        @pl.loop(0, chunks)
        def _(c):
            to_right(c).wait_send()

        @pl.loop(0, per_owner)
        def _(c):
            to_owner(c, last).wait_recv()

    @pl.when(me == last)
    def _():
        @pl.loop(0, chunks - per_owner)
        def _(c):
            to_owner(c, 0).wait_send()


def prompt_part(lengths, query, key, value, decay):
    n = lax.axis_size("seq")
    _, block, width = query.shape
    heads = width // HEAD_DIM
    share = heads // n
    chunk = min(CHUNK, share)
    vmem = pl.BlockSpec(memory_space=pltpu.VMEM)
    return pl.pallas_call(
        functools.partial(prompt_kernel, n, heads, block),
        out_shape=(
            jax.ShapeDtypeStruct(query.shape, BF16),
            jax.ShapeDtypeStruct((share, HEAD_DIM, HEAD_DIM), F32),
        ),
        in_specs=[pl.BlockSpec(memory_space=pltpu.SMEM)] + [vmem] * 4,
        out_specs=(vmem, vmem),
        scratch_shapes=[
            pltpu.VMEM((heads, block, HEAD_DIM), F32),
            pltpu.VMEM((heads, 1, block), F32),
            pltpu.VMEM((heads, 1, HEAD_DIM), F32),
            pltpu.VMEM((heads, HEAD_DIM, HEAD_DIM), F32),
            pltpu.VMEM((heads, HEAD_DIM, HEAD_DIM), F32),
            pltpu.VMEM((block, width), F32),
            pltpu.VMEM((block, HEAD_DIM), F32),
            pltpu.VMEM((block, HEAD_DIM), F32),
            pltpu.SemaphoreType.DMA((heads // chunk,)),
            pltpu.SemaphoreType.DMA((heads // chunk,)),
            pltpu.SemaphoreType.DMA((heads // chunk,)),
            pltpu.SemaphoreType.DMA((share // chunk,)),
        ],
        compiler_params=pltpu.CompilerParams(
            collective_id=0, has_side_effects=True, vmem_limit_bytes=52 * 1024 * 1024
        ),
    )(lengths, query, key, value, decay)


def shards(
    lengths,
    prompt_query,
    prompt_key,
    prompt_value,
    prompt_decay,
    step_query,
    step_key,
    step_value,
    step_decay,
    out_weight,
):
    feat_width = prompt_query.shape[2]
    prompt_out, final_state = prompt_part(
        lengths, prompt_query, prompt_key, prompt_value, prompt_decay
    )
    steps, reqs, part_width = step_query.shape
    share = part_width // HEAD_DIM
    shape = (steps, share, HEAD_DIM)
    q = step_query.reshape(shape).astype(F32)
    k = step_key.reshape(shape).astype(F32)
    v = step_value.reshape(shape).astype(F32)
    high = lax.Precision.HIGHEST
    at = jnp.arange(steps)
    causal = (at[:, None] >= at[None, :])[:, :, None]
    cum = jnp.sum(jnp.where(causal, step_decay.reshape(steps, share)[None], 0.0), axis=1)
    gaps = jnp.where(causal, cum[:, None, :] - cum[None, :, :], 0.0)
    weights = jnp.where(causal, jnp.exp(gaps), 0.0)
    own = jnp.sum(q[:, None] * k[None, :], axis=-1) * weights
    fresh = jnp.sum(own[:, :, :, None] * v[None, :], axis=1)
    kept = jnp.einsum("shk,hkv->shv", q, final_state, precision=high)
    heard = (kept * jnp.exp(cum)[:, :, None] + fresh).reshape(steps, reqs, part_width)
    sum_squares = lax.psum(jnp.sum(heard * heard, axis=-1), "seq")
    normed = (heard * lax.rsqrt(sum_squares[:, :, None] / feat_width + epsilon)).astype(BF16)
    projected = jnp.einsum(
        "srf,fc->src",
        lax.all_gather(normed, "rep", axis=1, tiled=True),
        out_weight,
        preferred_element_type=F32,
    )
    step_out = lax.psum(projected, "seq").astype(BF16)
    return (prompt_out, step_out)


def solution(mesh):
    return jax.shard_map(
        shards,
        mesh=mesh,
        in_specs=(
            P("rep"),
            P("rep", "seq", None),
            P("rep", "seq", None),
            P("rep", "seq", None),
            P("rep", None, "seq"),
            P(None, "rep", "seq"),
            P(None, "rep", "seq"),
            P(None, "rep", "seq"),
            P(None, "rep", "seq"),
            P("seq", "rep"),
        ),
        out_specs=(P("rep", "seq", None), P(None, None, "rep")),
        check_vma=False,
    )
```

time: 292 us -> 114 us (0.39)
  waiting for transfers between devices: 109 us -> 0 us
  other arithmetic: 41.3 us -> 1.14 us
  matrix products: 38.3 us -> 0.68 us
  Pallas kernels: 0 us -> 35.3 us
  local copies, waits for them, and re-layouts: 20.8 us -> 6.91 us
  between operations: 15 us -> 1.46 us
    all_gather x1 -> x0, waiting for transfers between devices: 93.6 us -> none  [entering(): everything = jax.tree.map(lambda part: lax.all_gather(part, axis), array)]
    dot_general x7 -> x1, matrix products: 38 us -> 0.35 us  [shards(): kept = jnp.einsum('shk,hkv->shv', q, final_state, precision=high)]
    pallas_call x0 -> x1, Pallas kernels: none -> 35.3 us  [prompt_part(): pl.pallas_call(functools.partial(prompt_kernel, n, heads, block), out_sha...]
    select_n x16 -> x0, other arithmetic: 30.5 us -> none  [hop(): return jax.tree.map(lambda a, b: jnp.where(reached, a, b), new, before)]
    psum x2, blocking collectives: 45.2 us -> 60.3 us  [the longest x1 33 us: shards(): sum_squares = lax.psum(jnp.sum(heard * heard, axis=-1), 'seq')]
    reduce_scatter x1 -> x0, waiting for transfers between devices: 14.5 us -> none  [shards(): lax.psum_scatter(block_local_state * jnp.exp(later_decay)[:, :, None, Non...]
    all_gather x1 -> x0, blocking collectives: 13.4 us -> none  [entering(): everything = jax.tree.map(lambda part: lax.all_gather(part, axis), array)]
    reshape x2 -> x1, local copies, waits for them, and re-layouts: 11.2 us -> 0.7 us  [shards(): q = step_query.reshape(shape).astype(F32)]
  transfers between devices with their start and end apart: 2 -> 0, of which waited for: 2 -> 0; matrix products, arithmetic and copies ran while one was open for 9% -> 0% of each run, Pallas kernels for 0% -> 0%
where the time goes in v1:
time: 114 us
  blocking collectives  68.5 us (60%)
  Pallas kernels  35.3 us (31%)
  local copies, waits for them, and re-layouts  6.91 us (6%)
  between operations  1.46 us (1%)
    pallas_call x1, Pallas kernels, prompt_part(): pl.pallas_call(functools.partial(prompt_kernel, n, heads, block), out_sha...  35.3 us
    psum x1, blocking collectives, shards(): sum_squares = lax.psum(jnp.sum(heard * heard, axis=-1), 'seq')  33 us
    psum x1, blocking collectives, shards(): step_out = lax.psum(projected, 'seq').astype(BF16)  27.3 us
    all_gather x1, blocking collectives, shards(): lax.all_gather(normed, 'rep', axis=1, tiled=True)  8.16 us
    unnamed x7, local copies, waits for them, and re-layouts  4.71 us

profile of v1, /device:TPU:0, one launch (start us, length us, event | category | flops | bytes accessed | tf_op | source)
XLA Modules:
  0.0 113.9 jit_solution(7435644278477203868)
XLA Ops:
  0.6 0.0 copy-start
  1.4 0.8 select_reduce_fusion
  2.2 0.1 copy.24
  2.3 0.7 reshape.113
  3.0 0.7 reshape.115
  3.7 0.1 multiply_reduce_fusion.1
  3.8 0.1 select_multiply_fusion
  3.9 0.7 reshape.116
  4.6 0.1 multiply_reduce_fusion
  4.7 0.0 copy-start.1
  4.7 0.8 copy-done.1
  5.5 0.0 copy-start.2
  5.5 35.3 %shard_map.113 = (bf16[1,384,4096]{2,1,0:T(8,128)(2,1)}, f32[4,128,128]{2,1,0:T(8,128)S(1)}) custom-call(s32[1]{0:T(128)S(6)} %copy.31.len_ref, bf16[1,384,4096]{2,1,0:T(8,128)(2,1)} %q_ref.1, bf16[1,384,4096]{2,1,0:T(8,128)(2,1)} %k_ref.1, bf16[1,384,4096]{2,1,0:T(8,128)(2,1)} %v_ref.1, f32[1,32,384]{2,1,0:T(8,128)S(1)} %copy-done.1), custom_call_target="tpu_custom_call" | custom-call | tf_op jit(solution)/shard_map/pallas_call | solution.py:198
  40.8 0.0 copy-done.2
  40.8 0.4 multiply_reduce_fusion.2
  41.2 33.0 %psum.14 = f32[4,1]{0,1:T(1,128)S(1)} all-reduce(f32[4,1]{0,1:T(1,128)S(1)} %bitcast.30), channel_id=1, replica_groups=mesh['seq'=8,'rep'=4] {'seq'}, use_global_device_ids=true, to_apply=%region_4.5 | all-reduce | flops 4 | bytes 32 | tf_op jit(solution)/shard_map/psum | solution.py:258
  74.1 0.1 fusion.5
  74.2 8.2 %all_gather.3 = bf16[4,4,512]{2,0,1:T(4,128)(2,1)S(1)} all-gather(bf16[4,1,512]{2,0,1:T(4,128)(2,1)S(1)} %fusion.5), channel_id=1, replica_groups=mesh['seq'=8,'rep'=4] {'rep'}, dimensions={1}, use_global_device_ids=true | all-gather | bytes 20480 | tf_op jit(solution)/shard_map/all_gather | solution.py:262
  82.3 0.0 copy-done
  82.4 0.3 fusion
  82.7 27.3 %psum.15 = bf16[4,4,1536]{2,1,0:T(4,128)(2,1)} all-reduce(f32[4,4,1536]{2,1,0:T(4,128)S(1)} %fusion), channel_id=1, replica_groups=mesh['seq'=8,'rep'=4] {'seq'}, use_global_device_ids=true, to_apply=%region_5.6 | all-reduce | flops 24576 | bytes 147456 | tf_op jit(solution)/shard_map/psum | solution.py:266
  110.0 3.9 %copy.32 = bf16[1,384,4096]{2,1,0:T(8,128)(2,1)} copy(bf16[1,384,4096]{2,1,0:T(8,128)(2,1)} %get-tuple-element.10) | data formatting | bytes 6291456
  (4 shorter events, 0.0 us)
Async XLA Ops:
  0.6 81.7 %copy-start = (bf16[512,1536]{1,0:T(8,128)(2,1)S(1)}, bf16[512,1536]{1,0:T(8,128)(2,1)}, u32[]{:S(2)}) copy-start(bf16[512,1536]{1,0:T(8,128)(2,1)} %param.19) | copy-start | bytes 4718596
  4.7 0.8 copy-start.1
  5.5 35.3 %copy-start.2 = (bf16[4,1,512]{2,0,1:T(4,128)(2,1)S(1)}, bf16[4,1,512]{2,0,1:T(4,128)(2,1)}, u32[]{:S(2)}) copy-start(bf16[4,1,512]{2,0,1:T(4,128)(2,1)} %param.15) | copy-start | bytes 12292

commit v2 on v1

--- a/solution.py
+++ b/solution.py
@@ -21,11 +21,13 @@
 
 
 def prompt_kernel(
-    n, heads, block,
-    len_ref, q_ref, k_ref, v_ref, d_ref,
-    out_ref, fin_ref,
+    n, reps, heads, block,
+    len_ref, q_ref, k_ref, v_ref, d_ref, sq_ref, sk_ref, sv_ref, sd_ref, w_ref,
+    out_ref, step_ref,
+    fin_ref, heard, ssq_all, norm_all, rows_in, parts, parts_in, sums, rows_out,
     cum_b, cum_row, total, state, inbox, attended, squares, live_b,
     send_sem, recv_sem, fin_send, fin_recv,
+    ssq_send, ssq_recv, norm_send, norm_recv, part_send, part_recv, sum_send, sum_recv,
 ):
     me = lax.axis_index("seq")
     rep = lax.axis_index("rep")
@@ -39,6 +41,11 @@
     for step in range(1, n):
         pl.semaphore_signal(
             barrier, inc=1, device_id=(lax.rem(me + step, n), rep), device_id_type=MESH
+        )
+
+    for step in range(1, reps):
+        pl.semaphore_signal(
+            barrier, inc=1, device_id=(me, lax.rem(rep + step, reps)), device_id_type=MESH
         )
 
     length = len_ref[0]
@@ -84,7 +91,7 @@
             device_id_type=MESH,
         )
 
-    pl.semaphore_wait(barrier, n - 1)
+    pl.semaphore_wait(barrier, n - 1 + reps - 1)
 
     @pl.loop(0, chunks)
     def _(c):
@@ -167,9 +174,105 @@
         scale = jnp.broadcast_to(lax.rsqrt(mean + epsilon), (tile, HEAD_DIM)) * live_b[rows, :]
         squares[rows, :] = scale
 
-    @pl.loop(0, heads)
-    def _(h):
-        out_ref[0, :, columns(h)] = (attended[:, columns(h)] * squares[...]).astype(BF16)
+    def scale_out(first, end):
+        @pl.loop(first, end)
+        def _(h):
+            out_ref[0, :, columns(h)] = (attended[:, columns(h)] * squares[...]).astype(BF16)
+
+    def along_seq(source, target, sends, receives, step, slot, arriving):
+        peer = lax.rem(me + step, n)
+        landing = peer if arriving else me
+        return pltpu.make_async_remote_copy(
+            src_ref=source.at[peer if slot else me],
+            dst_ref=target.at[landing],
+            send_sem=sends.at[step],
+            recv_sem=receives.at[landing],
+            device_id=(peer, rep),
+            device_id_type=MESH,
+        )
+
+    def along_rep(step, arriving):
+        peer = lax.rem(rep + step, reps)
+        landing = peer if arriving else rep
+        return pltpu.make_async_remote_copy(
+            src_ref=norm_all.at[rep],
+            dst_ref=norm_all.at[landing],
+            send_sem=norm_send.at[step],
+            recv_sem=norm_recv.at[landing],
+            device_id=(me, peer),
+            device_id_type=MESH,
+        )
+
+    @pl.when(me < last)
+    def _():
+        @pl.loop(0, per_owner)
+        def _(c):
+            to_owner(c, last).wait_recv()
+
+    steps = sq_ref.shape[0]
+    heard[...] = jnp.zeros_like(heard)
+    for i in range(share):
+        cols = slice(i * HEAD_DIM, (i + 1) * HEAD_DIM)
+        queries = [sq_ref[s, :, cols].astype(F32) for s in range(steps)]
+        keys = [sk_ref[s, :, cols].astype(F32) for s in range(steps)]
+        values = [sv_ref[s, :, cols].astype(F32) for s in range(steps)]
+        cums = []
+        for s in range(steps):
+            one = sd_ref[s, :, i : i + 1]
+            cums.append(one if s == 0 else cums[-1] + one)
+        for s in range(steps):
+            heard[s : s + 1, cols] = queries[s]
+        kept = dot(heard[:, cols], fin_ref[i], 1, 0, lax.Precision.HIGHEST)
+        for s in range(steps):
+            row = jnp.exp(cums[s]) * kept[s : s + 1, :]
+            for j in range(s + 1):
+                meet = jnp.sum(queries[s] * keys[j], axis=1, keepdims=True)
+                row = row + (meet * jnp.exp(cums[s] - cums[j])) * values[j]
+            heard[s : s + 1, cols] = row
+    mine = heard[:steps, :]
+    ssq_all[me] = jnp.broadcast_to(jnp.sum(mine * mine, axis=1, keepdims=True), (steps, HEAD_DIM))
+    for step in range(1, n):
+        along_seq(ssq_all, ssq_all, ssq_send, ssq_recv, step, False, False).start()
+    cut = heads // 3
+    scale_out(0, cut)
+    for step in range(1, n):
+        along_seq(ssq_all, ssq_all, ssq_send, ssq_recv, step, False, True).wait_recv()
+    mean = jnp.sum(ssq_all[...], axis=0)[:, :1] / (heads * HEAD_DIM)
+    norm_all[rep] = (mine * lax.rsqrt(mean + epsilon)).astype(BF16).astype(F32)
+    for step in range(1, reps):
+        along_rep(step, False).start()
+    scale_out(cut, 2 * cut)
+    for step in range(1, reps):
+        along_rep(step, True).wait_recv()
+    for r in range(reps):
+        for s in range(steps):
+            at = s * reps + r
+            rows_in[at : at + 1, :] = norm_all[r, s : s + 1, :]
+    projected = dot(rows_in[...].astype(BF16), w_ref[...], 1, 0)
+    per = steps * reps // n
+    for j in range(n):
+        parts[j] = projected[j * per : (j + 1) * per, :]
+    for step in range(1, n):
+        along_seq(parts, parts_in, part_send, part_recv, step, True, False).start()
+    parts_in[me] = parts[me]
+    scale_out(2 * cut, heads)
+    for step in range(1, n):
+        along_seq(parts, parts_in, part_send, part_recv, step, True, True).wait_recv()
+    sums[me] = jnp.sum(parts_in[...], axis=0)
+    for step in range(1, n):
+        along_seq(sums, sums, sum_send, sum_recv, step, False, False).start()
+    for step in range(1, n):
+        along_seq(sums, sums, sum_send, sum_recv, step, False, True).wait_recv()
+    for j in range(n):
+        rows_out[j * per : (j + 1) * per, :] = sums[j]
+    step_ref[...] = rows_out[...].astype(BF16)
+
+    for step in range(1, n):
+        along_seq(ssq_all, ssq_all, ssq_send, ssq_recv, step, False, False).wait_send()
+        along_seq(parts, parts_in, part_send, part_recv, step, True, False).wait_send()
+        along_seq(sums, sums, sum_send, sum_recv, step, False, False).wait_send()
+    for step in range(1, reps):
+        along_rep(step, False).wait_send()
 
     @pl.when(me < last)
     def _():
@@ -177,10 +280,6 @@
         def _(c):
             to_right(c).wait_send()
 
-        @pl.loop(0, per_owner)
-        def _(c):
-            to_owner(c, last).wait_recv()
-
     @pl.when(me == last)
     def _():
         @pl.loop(0, chunks - per_owner)
@@ -188,22 +287,34 @@
             to_owner(c, 0).wait_send()
 
 
-def prompt_part(lengths, query, key, value, decay):
-    n = lax.axis_size("seq")
+def whole(lengths, query, key, value, decay, *decoding):
+    n, reps = lax.axis_size("seq"), lax.axis_size("rep")
     _, block, width = query.shape
     heads = width // HEAD_DIM
     share = heads // n
     chunk = min(CHUNK, share)
+    steps, _, part_width = decoding[0].shape
+    out_columns = decoding[-1].shape[1]
+    rows = steps * reps
     vmem = pl.BlockSpec(memory_space=pltpu.VMEM)
     return pl.pallas_call(
-        functools.partial(prompt_kernel, n, heads, block),
+        functools.partial(prompt_kernel, n, reps, heads, block),
         out_shape=(
             jax.ShapeDtypeStruct(query.shape, BF16),
-            jax.ShapeDtypeStruct((share, HEAD_DIM, HEAD_DIM), F32),
+            jax.ShapeDtypeStruct((rows, out_columns), BF16),
         ),
-        in_specs=[pl.BlockSpec(memory_space=pltpu.SMEM)] + [vmem] * 4,
+        in_specs=[pl.BlockSpec(memory_space=pltpu.SMEM)] + [vmem] * 9,
         out_specs=(vmem, vmem),
         scratch_shapes=[
+            pltpu.VMEM((share, HEAD_DIM, HEAD_DIM), F32),
+            pltpu.VMEM((8 * pl.cdiv(steps, 8), part_width), F32),
+            pltpu.VMEM((n, steps, HEAD_DIM), F32),
+            pltpu.VMEM((reps, steps, part_width), F32),
+            pltpu.VMEM((rows, part_width), F32),
+            pltpu.VMEM((n, rows // n, out_columns), F32),
+            pltpu.VMEM((n, rows // n, out_columns), F32),
+            pltpu.VMEM((n, rows // n, out_columns), F32),
+            pltpu.VMEM((rows, out_columns), F32),
             pltpu.VMEM((heads, block, HEAD_DIM), F32),
             pltpu.VMEM((heads, 1, block), F32),
             pltpu.VMEM((heads, 1, HEAD_DIM), F32),
@@ -216,11 +327,19 @@
             pltpu.SemaphoreType.DMA((heads // chunk,)),
             pltpu.SemaphoreType.DMA((heads // chunk,)),
             pltpu.SemaphoreType.DMA((share // chunk,)),
+            pltpu.SemaphoreType.DMA((n,)),
+            pltpu.SemaphoreType.DMA((n,)),
+            pltpu.SemaphoreType.DMA((reps,)),
+            pltpu.SemaphoreType.DMA((reps,)),
+            pltpu.SemaphoreType.DMA((n,)),
+            pltpu.SemaphoreType.DMA((n,)),
+            pltpu.SemaphoreType.DMA((n,)),
+            pltpu.SemaphoreType.DMA((n,)),
         ],
         compiler_params=pltpu.CompilerParams(
             collective_id=0, has_side_effects=True, vmem_limit_bytes=52 * 1024 * 1024
         ),
-    )(lengths, query, key, value, decay)
+    )(lengths, query, key, value, decay, *decoding)
 
 
 def shards(
@@ -235,36 +354,20 @@
     step_decay,
     out_weight,
 ):
-    feat_width = prompt_query.shape[2]
-    prompt_out, final_state = prompt_part(
-        lengths, prompt_query, prompt_key, prompt_value, prompt_decay
+    prompt_out, rows = whole(
+        lengths,
+        prompt_query,
+        prompt_key,
+        prompt_value,
+        prompt_decay,
+        step_query,
+        step_key,
+        step_value,
+        step_decay,
+        out_weight,
     )
-    steps, reqs, part_width = step_query.shape
-    share = part_width // HEAD_DIM
-    shape = (steps, share, HEAD_DIM)
-    q = step_query.reshape(shape).astype(F32)
-    k = step_key.reshape(shape).astype(F32)
-    v = step_value.reshape(shape).astype(F32)
-    high = lax.Precision.HIGHEST
-    at = jnp.arange(steps)
-    causal = (at[:, None] >= at[None, :])[:, :, None]
-    cum = jnp.sum(jnp.where(causal, step_decay.reshape(steps, share)[None], 0.0), axis=1)
-    gaps = jnp.where(causal, cum[:, None, :] - cum[None, :, :], 0.0)
-    weights = jnp.where(causal, jnp.exp(gaps), 0.0)
-    own = jnp.sum(q[:, None] * k[None, :], axis=-1) * weights
-    fresh = jnp.sum(own[:, :, :, None] * v[None, :], axis=1)
-    kept = jnp.einsum("shk,hkv->shv", q, final_state, precision=high)
-    heard = (kept * jnp.exp(cum)[:, :, None] + fresh).reshape(steps, reqs, part_width)
-    sum_squares = lax.psum(jnp.sum(heard * heard, axis=-1), "seq")
-    normed = (heard * lax.rsqrt(sum_squares[:, :, None] / feat_width + epsilon)).astype(BF16)
-    projected = jnp.einsum(
-        "srf,fc->src",
-        lax.all_gather(normed, "rep", axis=1, tiled=True),
-        out_weight,
-        preferred_element_type=F32,
-    )
-    step_out = lax.psum(projected, "seq").astype(BF16)
-    return (prompt_out, step_out)
+    steps = step_query.shape[0]
+    return (prompt_out, rows.reshape(steps, rows.shape[0] // steps, rows.shape[1]))
 
 
 def solution(mesh):

time: 114 us -> 79.7 us (0.70)
  blocking collectives: 68.5 us -> 0 us
  Pallas kernels: 35.3 us -> 68.6 us
  local copies, waits for them, and re-layouts: 6.91 us -> 9.51 us
    psum x2 -> x0, blocking collectives: 60.3 us -> none  [the longest x1 33 us: shards(): sum_squares = lax.psum(jnp.sum(heard * heard, axis=-1), 'seq')]
    pallas_call x1, Pallas kernels: 35.3 us -> 68.6 us  [whole(): pl.pallas_call(functools.partial(prompt_kernel, n, reps, heads, block), o...]
    all_gather x1 -> x0, blocking collectives: 8.16 us -> none  [shards(): lax.all_gather(normed, 'rep', axis=1, tiled=True)]
    unnamed x7 -> x10, local copies, waits for them, and re-layouts: 4.71 us -> 8.87 us
    convert_element_type x2 -> x0, local copies, waits for them, and re-layouts: 1.39 us -> none  [the longest x1 0.7 us: shards(): v = step_value.reshape(shape).astype(F32)]
where the time goes in v2:
time: 79.7 us; the launch traced here: 79.4 us
  Pallas kernels  68.6 us (86%)
  local copies, waits for them, and re-layouts  9.51 us (12%)
  between operations  1.29 us (2%)
    pallas_call x1, Pallas kernels, whole(): pl.pallas_call(functools.partial(prompt_kernel, n, reps, heads, block), o...  68.6 us
    unnamed x10, local copies, waits for them, and re-layouts  8.87 us

profile of v2, /device:TPU:0, one launch (start us, length us, event | category | flops | bytes accessed | tf_op | source)
XLA Modules:
  0.0 79.4 jit_solution(5858998401115209412)
XLA Ops:
  1.3 0.7 copy.12.sq_ref
  2.0 0.7 copy.13.sk_ref
  2.7 0.7 copy.14.sv_ref
  3.4 0.0 copy-start
  3.4 1.4 %copy-done = bf16[512,1536]{1,0:T(8,128)(2,1)S(1)} copy-done((bf16[512,1536]{1,0:T(8,128)(2,1)S(1)}, bf16[512,1536]{1,0:T(8,128)(2,1)}, u32[]{:S(2)}) %copy-start) | copy-done | bytes 1572888
  4.8 0.0 copy-start.1
  4.8 0.8 %copy-done.1 = f32[1,32,384]{2,1,0:T(8,128)S(1)} copy-done((f32[1,32,384]{2,1,0:T(8,128)S(1)}, f32[1,32,384]{2,1,0:T(8,128)}, u32[]{:S(2)}) %copy-start.1) | copy-done | bytes 49176
  5.6 0.0 copy-start.2
  5.6 0.7 copy-done.2
  6.2 68.6 %shard_map.113 = (bf16[1,384,4096]{2,1,0:T(8,128)(2,1)}, bf16[16,1536]{1,0:T(8,128)(2,1)S(1)}) custom-call(s32[1]{0:T(128)S(6)} %copy.16.len_ref, bf16[1,384,4096]{2,1,0:T(8,128)(2,1)} %q_ref.1, bf16[1,384,4096]{2,1,0:T(8,128)(2,1)} %k_ref.1, bf16[1,384,4096]{2,1,0:T(8,128)(2,1)} %v_ref.1, f32[1,32,384]{2,1,0:T(8,128)S(1)} %copy-done.1, ...), custom_call_target="tpu_custom_call" | custom-call | tf_op jit(solution)/shard_map/pallas_call | solution.py:300
  74.8 0.6 reshape.7
  75.5 3.9 %copy.17 = bf16[1,384,4096]{2,1,0:T(8,128)(2,1)} copy(bf16[1,384,4096]{2,1,0:T(8,128)(2,1)} %get-tuple-element.8) | data formatting | bytes 6291456
Async XLA Ops:
  3.4 1.4 %copy-start = (bf16[512,1536]{1,0:T(8,128)(2,1)S(1)}, bf16[512,1536]{1,0:T(8,128)(2,1)}, u32[]{:S(2)}) copy-start(bf16[512,1536]{1,0:T(8,128)(2,1)} %w_ref.1) | copy-start | bytes 4718596
  4.8 0.8 %copy-start.1 = (f32[1,32,384]{2,1,0:T(8,128)S(1)}, f32[1,32,384]{2,1,0:T(8,128)}, u32[]{:S(2)}) copy-start(f32[1,32,384]{2,1,0:T(8,128)} %d_ref.1) | copy-start | bytes 147460
  5.6 0.7 copy-start.2

commit v3 on v2

--- a/solution.py
+++ b/solution.py
@@ -7,7 +7,7 @@
 from jax.sharding import PartitionSpec as P
 
 HEAD_DIM = 128
-CHUNK = 2
+CHUNK = 1
 epsilon = 1e-06
 MESH = pl.DeviceIdType.MESH
 F32 = jnp.float32
@@ -22,8 +22,9 @@
 
 def prompt_kernel(
     n, reps, heads, block,
-    len_ref, q_ref, k_ref, v_ref, d_ref, sq_ref, sk_ref, sv_ref, sd_ref, w_ref,
+    len_ref, q_hbm, k_hbm, v_hbm, d_hbm, step_in, sd_ref, w_hbm,
     out_ref, step_ref,
+    q_ref, k_ref, v_ref, d_ref, w_ref, load_sem, gains, fresh,
     fin_ref, heard, ssq_all, norm_all, rows_in, parts, parts_in, sums, rows_out,
     cum_b, cum_row, total, state, inbox, attended, squares, live_b,
     send_sem, recv_sem, fin_send, fin_recv,
@@ -37,6 +38,20 @@
     chunks = heads // chunk
     per_owner = share // chunk
 
+    loads = [
+        pltpu.make_async_copy(source, target, load_sem.at[i])
+        for i, (source, target) in enumerate(
+            (
+                (d_hbm, d_ref),
+                (k_hbm, k_ref),
+                (v_hbm, v_ref),
+                (q_hbm, q_ref),
+                (w_hbm, w_ref),
+            )
+        )
+    ]
+    for load in loads:
+        load.start()
     barrier = pltpu.get_barrier_semaphore()
     for step in range(1, n):
         pl.semaphore_signal(
@@ -54,6 +69,7 @@
     live_b[...] = (
         lax.broadcasted_iota(jnp.int32, (block, HEAD_DIM), 0) + start < length
     ).astype(F32)
+    loads[0].wait()
     log_decay = d_ref[0] * row_live
     below = (
         lax.broadcasted_iota(jnp.int32, (block, block), 0)
@@ -91,6 +107,8 @@
             device_id_type=MESH,
         )
 
+    loads[1].wait()
+    loads[2].wait()
     pl.semaphore_wait(barrier, n - 1 + reps - 1)
 
     @pl.loop(0, chunks)
@@ -104,6 +122,27 @@
         @pl.when(me == 0)
         def _():
             to_right(c).start()
+
+    loads[3].wait()
+    loads[4].wait()
+    steps = step_in.shape[0] // 3
+    heard[...] = jnp.zeros_like(heard)
+    gains[...] = jnp.zeros_like(gains)
+    fresh[...] = jnp.zeros_like(fresh)
+    heard[:steps, :] = step_in[:steps, :]
+    for i in range(share):
+        cols = slice(i * HEAD_DIM, (i + 1) * HEAD_DIM)
+        cums = []
+        for s in range(steps):
+            one = sd_ref[s, :, i : i + 1]
+            cums.append(one if s == 0 else cums[-1] + one)
+            row = jnp.zeros((1, HEAD_DIM), F32)
+            for j in range(s + 1):
+                met = step_in[s : s + 1, cols] * step_in[steps + j : steps + j + 1, cols]
+                meet = jnp.sum(met, axis=1, keepdims=True) * jnp.exp(cums[s] - cums[j])
+                row = row + meet * step_in[2 * steps + j : 2 * steps + j + 1, cols]
+            fresh[s : s + 1, cols] = row
+            gains[s : s + 1, cols] = jnp.broadcast_to(jnp.exp(cums[s]), (1, HEAD_DIM))
 
     tile = HEAD_DIM
     tiles = block // tile
@@ -209,26 +248,10 @@
         def _(c):
             to_owner(c, last).wait_recv()
 
-    steps = sq_ref.shape[0]
-    heard[...] = jnp.zeros_like(heard)
     for i in range(share):
         cols = slice(i * HEAD_DIM, (i + 1) * HEAD_DIM)
-        queries = [sq_ref[s, :, cols].astype(F32) for s in range(steps)]
-        keys = [sk_ref[s, :, cols].astype(F32) for s in range(steps)]
-        values = [sv_ref[s, :, cols].astype(F32) for s in range(steps)]
-        cums = []
-        for s in range(steps):
-            one = sd_ref[s, :, i : i + 1]
-            cums.append(one if s == 0 else cums[-1] + one)
-        for s in range(steps):
-            heard[s : s + 1, cols] = queries[s]
         kept = dot(heard[:, cols], fin_ref[i], 1, 0, lax.Precision.HIGHEST)
-        for s in range(steps):
-            row = jnp.exp(cums[s]) * kept[s : s + 1, :]
-            for j in range(s + 1):
-                meet = jnp.sum(queries[s] * keys[j], axis=1, keepdims=True)
-                row = row + (meet * jnp.exp(cums[s] - cums[j])) * values[j]
-            heard[s : s + 1, cols] = row
+        heard[:, cols] = gains[:, cols] * kept + fresh[:, cols]
     mine = heard[:steps, :]
     ssq_all[me] = jnp.broadcast_to(jnp.sum(mine * mine, axis=1, keepdims=True), (steps, HEAD_DIM))
     for step in range(1, n):
@@ -287,14 +310,16 @@
             to_owner(c, 0).wait_send()
 
 
-def whole(lengths, query, key, value, decay, *decoding):
+def whole(lengths, query, key, value, decay, step_in, step_decay, weight):
     n, reps = lax.axis_size("seq"), lax.axis_size("rep")
     _, block, width = query.shape
     heads = width // HEAD_DIM
     share = heads // n
     chunk = min(CHUNK, share)
-    steps, _, part_width = decoding[0].shape
-    out_columns = decoding[-1].shape[1]
+    steps, part_width = step_decay.shape[0], step_in.shape[1]
+    out_columns = weight.shape[1]
+    padded = 8 * pl.cdiv(steps, 8)
+    hbm = pl.BlockSpec(memory_space=pltpu.HBM)
     rows = steps * reps
     vmem = pl.BlockSpec(memory_space=pltpu.VMEM)
     return pl.pallas_call(
@@ -303,11 +328,19 @@
             jax.ShapeDtypeStruct(query.shape, BF16),
             jax.ShapeDtypeStruct((rows, out_columns), BF16),
         ),
-        in_specs=[pl.BlockSpec(memory_space=pltpu.SMEM)] + [vmem] * 9,
+        in_specs=[pl.BlockSpec(memory_space=pltpu.SMEM)] + [hbm] * 4 + [vmem] * 2 + [hbm],
         out_specs=(vmem, vmem),
         scratch_shapes=[
+            pltpu.VMEM(query.shape, BF16),
+            pltpu.VMEM(key.shape, BF16),
+            pltpu.VMEM(value.shape, BF16),
+            pltpu.VMEM(decay.shape, F32),
+            pltpu.VMEM(weight.shape, BF16),
+            pltpu.SemaphoreType.DMA((5,)),
+            pltpu.VMEM((padded, part_width), F32),
+            pltpu.VMEM((padded, part_width), F32),
             pltpu.VMEM((share, HEAD_DIM, HEAD_DIM), F32),
-            pltpu.VMEM((8 * pl.cdiv(steps, 8), part_width), F32),
+            pltpu.VMEM((padded, part_width), F32),
             pltpu.VMEM((n, steps, HEAD_DIM), F32),
             pltpu.VMEM((reps, steps, part_width), F32),
             pltpu.VMEM((rows, part_width), F32),
@@ -337,9 +370,9 @@
             pltpu.SemaphoreType.DMA((n,)),
         ],
         compiler_params=pltpu.CompilerParams(
-            collective_id=0, has_side_effects=True, vmem_limit_bytes=52 * 1024 * 1024
+            collective_id=0, has_side_effects=True, vmem_limit_bytes=63 * 1024 * 1024
         ),
-    )(lengths, query, key, value, decay, *decoding)
+    )(lengths, query, key, value, decay, step_in, step_decay, weight)
 
 
 def shards(
@@ -354,15 +387,17 @@
     step_decay,
     out_weight,
 ):
+    wide = (-1, step_query.shape[2])
+    step_in = jnp.concatenate(
+        [part.reshape(wide).astype(F32) for part in (step_query, step_key, step_value)]
+    )
     prompt_out, rows = whole(
         lengths,
         prompt_query,
         prompt_key,
         prompt_value,
         prompt_decay,
-        step_query,
-        step_key,
-        step_value,
+        step_in,
         step_decay,
         out_weight,
     )

time: 79.7 us -> 75.5 us (0.947)
  local copies, waits for them, and re-layouts: 9.51 us -> 5.34 us
  Pallas kernels: 68.6 us -> 67.2 us
  other arithmetic: 0 us -> 1.34 us
    unnamed x10 -> x1, local copies, waits for them, and re-layouts: 8.87 us -> 3.91 us
    pallas_call x1, Pallas kernels: 68.6 us -> 67.2 us  [whole(): pl.pallas_call(functools.partial(prompt_kernel, n, reps, heads, block), o...]
    concatenate x0 -> x1, other arithmetic: none -> 1.34 us  [shards(): jnp.concatenate([part.reshape(wide).astype(F32) for part in (step_query,...]
    reshape x1, local copies, waits for them, and re-layouts: 0.64 us -> 1.44 us  [shards(): rows.reshape(steps, rows.shape[0] // steps, rows.shape[1])]
where the time goes in v3:
time: 75.5 us; the launch traced here: 75.2 us
  Pallas kernels  67.2 us (89%)
  local copies, waits for them, and re-layouts  5.34 us (7%)
  other arithmetic  1.34 us (2%)
  between operations  1.28 us (2%)
    pallas_call x1, Pallas kernels, whole(): pl.pallas_call(functools.partial(prompt_kernel, n, reps, heads, block), o...  67.2 us
    unnamed x1, local copies, waits for them, and re-layouts  3.91 us

profile of v3, /device:TPU:0, one launch (start us, length us, event | category | flops | bytes accessed | tf_op | source)
XLA Modules:
  0.0 75.2 jit_solution(8628728522034269364)
XLA Ops:
  1.3 1.3 %maximum_convert_fusion.step_in = f32[12,512]{1,0:T(8,128)} fusion(bf16[4,512]{1,0:T(4,128)(2,1)} %bitcast.3, bf16[4,512]{1,0:T(4,128)(2,1)} %bitcast.4, bf16[4,512]{1,0:T(4,128)(2,1)} %bitcast.5), kind=kLoop, calls=%fused_computation | loop fusion | flops 36864 | bytes 36864 | tf_op jit(solution)/shard_map/concatenate | solution.py:391
  2.6 67.2 %shard_map.113 = (bf16[1,384,4096]{2,1,0:T(8,128)(2,1)}, bf16[16,1536]{1,0:T(8,128)(2,1)}) custom-call(s32[1]{0:T(128)S(6)} %copy.13.len_ref, bf16[1,384,4096]{2,1,0:T(8,128)(2,1)} %q_hbm.1, bf16[1,384,4096]{2,1,0:T(8,128)(2,1)} %k_hbm.1, bf16[1,384,4096]{2,1,0:T(8,128)(2,1)} %v_hbm.1, f32[1,32,384]{2,1,0:T(8,128)} %d_hbm.1, ...), custom_call_target="tpu_custom_call" | custom-call | tf_op jit(solution)/shard_map/pallas_call | solution.py:325
  69.8 1.4 %reshape.16 = bf16[4,4,1536]{2,1,0:T(4,128)(2,1)} reshape(bf16[16,1536]{1,0:T(8,128)(2,1)} %get-tuple-element.5) | data formatting | bytes 98304 | tf_op jit(solution)/shard_map/reshape | solution.py:405
  71.3 3.9 %copy.14 = bf16[1,384,4096]{2,1,0:T(8,128)(2,1)} copy(bf16[1,384,4096]{2,1,0:T(8,128)(2,1)} %get-tuple-element.8) | data formatting | bytes 6291456

commit v4 on v3

--- a/solution.py
+++ b/solution.py
@@ -22,9 +22,9 @@
 
 def prompt_kernel(
     n, reps, heads, block,
-    len_ref, q_hbm, k_hbm, v_hbm, d_hbm, step_in, sd_ref, w_hbm,
+    len_ref, q_hbm, k_hbm, v_hbm, d_hbm, sq_ref, sk_ref, sv_ref, sd_ref, w_hbm,
     out_ref, step_ref,
-    q_ref, k_ref, v_ref, d_ref, w_ref, load_sem, gains, fresh,
+    q_ref, k_ref, v_ref, d_ref, w_ref, load_sem, gains, fresh, step_in,
     fin_ref, heard, ssq_all, norm_all, rows_in, parts, parts_in, sums, rows_out,
     cum_b, cum_row, total, state, inbox, attended, squares, live_b,
     send_sem, recv_sem, fin_send, fin_recv,
@@ -125,7 +125,9 @@
 
     loads[3].wait()
     loads[4].wait()
-    steps = step_in.shape[0] // 3
+    steps = sq_ref.shape[0]
+    for i, part in enumerate((sq_ref, sk_ref, sv_ref)):
+        step_in[i * steps : (i + 1) * steps, :] = part[...].astype(F32)
     heard[...] = jnp.zeros_like(heard)
     gains[...] = jnp.zeros_like(gains)
     fresh[...] = jnp.zeros_like(fresh)
@@ -156,8 +158,7 @@
     def _():
         inbox[...] = jnp.zeros_like(inbox)
 
-    @pl.loop(0, chunks)
-    def _(c):
+    def forward(c):
         @pl.when(me > 0)
         def _():
             to_right(c).wait_recv()
@@ -183,6 +184,7 @@
                         pl.ds(c * chunk, chunk)
                     ]
 
+    def attend(c):
         for i in range(chunk):
             h = c * chunk + i
             query = q_ref[0, :, columns(h)]
@@ -207,16 +209,20 @@
                 attended[rows, columns(h)] = both
                 squares[rows, :] += both * both
 
-    for t in range(tiles):
-        rows = slice(t * tile, (t + 1) * tile)
-        mean = jnp.sum(squares[rows, :], axis=1, keepdims=True) / (heads * HEAD_DIM)
-        scale = jnp.broadcast_to(lax.rsqrt(mean + epsilon), (tile, HEAD_DIM)) * live_b[rows, :]
-        squares[rows, :] = scale
-
-    def scale_out(first, end):
-        @pl.loop(first, end)
-        def _(h):
-            out_ref[0, :, columns(h)] = (attended[:, columns(h)] * squares[...]).astype(BF16)
+    half = chunks // 2
+    quarter = half // 4
+
+    @pl.loop(0, half)
+    def _(c):
+        forward(c)
+        attend(c)
+
+    @pl.loop(half, chunks)
+    def _(c):
+        forward(c)
+
+    def attend_part(part):
+        pl.loop(half + part * quarter, chunks if part == 3 else half + (part + 1) * quarter)(attend)
 
     def along_seq(source, target, sends, receives, step, slot, arriving):
         peer = lax.rem(me + step, n)
@@ -256,15 +262,14 @@
     ssq_all[me] = jnp.broadcast_to(jnp.sum(mine * mine, axis=1, keepdims=True), (steps, HEAD_DIM))
     for step in range(1, n):
         along_seq(ssq_all, ssq_all, ssq_send, ssq_recv, step, False, False).start()
-    cut = heads // 3
-    scale_out(0, cut)
+    attend_part(0)
     for step in range(1, n):
         along_seq(ssq_all, ssq_all, ssq_send, ssq_recv, step, False, True).wait_recv()
     mean = jnp.sum(ssq_all[...], axis=0)[:, :1] / (heads * HEAD_DIM)
     norm_all[rep] = (mine * lax.rsqrt(mean + epsilon)).astype(BF16).astype(F32)
     for step in range(1, reps):
         along_rep(step, False).start()
-    scale_out(cut, 2 * cut)
+    attend_part(1)
     for step in range(1, reps):
         along_rep(step, True).wait_recv()
     for r in range(reps):
@@ -278,17 +283,29 @@
     for step in range(1, n):
         along_seq(parts, parts_in, part_send, part_recv, step, True, False).start()
     parts_in[me] = parts[me]
-    scale_out(2 * cut, heads)
+    attend_part(2)
     for step in range(1, n):
         along_seq(parts, parts_in, part_send, part_recv, step, True, True).wait_recv()
     sums[me] = jnp.sum(parts_in[...], axis=0)
     for step in range(1, n):
         along_seq(sums, sums, sum_send, sum_recv, step, False, False).start()
+    attend_part(3)
+    for t in range(tiles):
+        rows = slice(t * tile, (t + 1) * tile)
+        mean = jnp.sum(squares[rows, :], axis=1, keepdims=True) / (heads * HEAD_DIM)
+        scale = jnp.broadcast_to(lax.rsqrt(mean + epsilon), (tile, HEAD_DIM)) * live_b[rows, :]
+        squares[rows, :] = scale
+
+    @pl.loop(0, heads)
+    def _(h):
+        out_ref[0, :, columns(h)] = (attended[:, columns(h)] * squares[...]).astype(BF16)
+
     for step in range(1, n):
         along_seq(sums, sums, sum_send, sum_recv, step, False, True).wait_recv()
     for j in range(n):
         rows_out[j * per : (j + 1) * per, :] = sums[j]
-    step_ref[...] = rows_out[...].astype(BF16)
+    for s in range(steps):
+        step_ref[s] = rows_out[s * reps : (s + 1) * reps, :].astype(BF16)
 
     for step in range(1, n):
         along_seq(ssq_all, ssq_all, ssq_send, ssq_recv, step, False, False).wait_send()
@@ -310,13 +327,13 @@
             to_owner(c, 0).wait_send()
 
 
-def whole(lengths, query, key, value, decay, step_in, step_decay, weight):
+def whole(lengths, query, key, value, decay, step_q, step_k, step_v, step_decay, weight):
     n, reps = lax.axis_size("seq"), lax.axis_size("rep")
     _, block, width = query.shape
     heads = width // HEAD_DIM
     share = heads // n
     chunk = min(CHUNK, share)
-    steps, part_width = step_decay.shape[0], step_in.shape[1]
+    steps, part_width = step_decay.shape[0], step_q.shape[1]
     out_columns = weight.shape[1]
     padded = 8 * pl.cdiv(steps, 8)
     hbm = pl.BlockSpec(memory_space=pltpu.HBM)
@@ -326,9 +343,9 @@
         functools.partial(prompt_kernel, n, reps, heads, block),
         out_shape=(
             jax.ShapeDtypeStruct(query.shape, BF16),
-            jax.ShapeDtypeStruct((rows, out_columns), BF16),
+            jax.ShapeDtypeStruct((steps, reps, out_columns), BF16),
         ),
-        in_specs=[pl.BlockSpec(memory_space=pltpu.SMEM)] + [hbm] * 4 + [vmem] * 2 + [hbm],
+        in_specs=[pl.BlockSpec(memory_space=pltpu.SMEM)] + [hbm] * 4 + [vmem] * 4 + [hbm],
         out_specs=(vmem, vmem),
         scratch_shapes=[
             pltpu.VMEM(query.shape, BF16),
@@ -339,6 +356,7 @@
             pltpu.SemaphoreType.DMA((5,)),
             pltpu.VMEM((padded, part_width), F32),
             pltpu.VMEM((padded, part_width), F32),
+            pltpu.VMEM((3 * steps, part_width), F32),
             pltpu.VMEM((share, HEAD_DIM, HEAD_DIM), F32),
             pltpu.VMEM((padded, part_width), F32),
             pltpu.VMEM((n, steps, HEAD_DIM), F32),
@@ -372,7 +390,7 @@
         compiler_params=pltpu.CompilerParams(
             collective_id=0, has_side_effects=True, vmem_limit_bytes=63 * 1024 * 1024
         ),
-    )(lengths, query, key, value, decay, step_in, step_decay, weight)
+    )(lengths, query, key, value, decay, step_q, step_k, step_v, step_decay, weight)
 
 
 def shards(
@@ -388,21 +406,19 @@
     out_weight,
 ):
     wide = (-1, step_query.shape[2])
-    step_in = jnp.concatenate(
-        [part.reshape(wide).astype(F32) for part in (step_query, step_key, step_value)]
-    )
-    prompt_out, rows = whole(
+    prompt_out, step_out = whole(
         lengths,
         prompt_query,
         prompt_key,
         prompt_value,
         prompt_decay,
-        step_in,
+        step_query.reshape(wide),
+        step_key.reshape(wide),
+        step_value.reshape(wide),
         step_decay,
         out_weight,
     )
-    steps = step_query.shape[0]
-    return (prompt_out, rows.reshape(steps, rows.shape[0] // steps, rows.shape[1]))
+    return (prompt_out, step_out)
 
 
 def solution(mesh):

time: 75.5 us -> 72.6 us (0.962)
  other arithmetic: 1.34 us -> 0 us
  local copies, waits for them, and re-layouts: 5.34 us -> 4.54 us
    reshape x1 -> x0, local copies, waits for them, and re-layouts: 1.44 us -> none  [shards(): rows.reshape(steps, rows.shape[0] // steps, rows.shape[1])]
    concatenate x1 -> x0, other arithmetic: 1.34 us -> none  [shards(): jnp.concatenate([part.reshape(wide).astype(F32) for part in (step_query,...]
    unnamed x1 -> x4, local copies, waits for them, and re-layouts: 3.91 us -> 4.54 us
where the time goes in v4:
time: 72.6 us; the launch traced here: 72.4 us
  Pallas kernels  66.6 us (92%)
  local copies, waits for them, and re-layouts  4.54 us (6%)
  between operations  1.3 us (2%)
    pallas_call x1, Pallas kernels, whole(): pl.pallas_call(functools.partial(prompt_kernel, n, reps, heads, block), o...  66.6 us
    unnamed x4, local copies, waits for them, and re-layouts  4.54 us

profile of v4, /device:TPU:0, one launch (start us, length us, event | category | flops | bytes accessed | tf_op | source)
XLA Modules:
  0.0 72.4 jit_solution(12834770214759635922)
XLA Ops:
  1.3 66.6 %shard_map.113 = (bf16[1,384,4096]{2,1,0:T(8,128)(2,1)}, bf16[4,4,1536]{2,1,0:T(4,128)(2,1)}) custom-call(s32[1]{0:T(128)S(6)} %copy.14.len_ref, bf16[1,384,4096]{2,1,0:T(8,128)(2,1)} %q_hbm.1, bf16[1,384,4096]{2,1,0:T(8,128)(2,1)} %k_hbm.1, bf16[1,384,4096]{2,1,0:T(8,128)(2,1)} %v_hbm.1, f32[1,32,384]{2,1,0:T(8,128)} %d_hbm.1, bf16[4,512]{1,0:T(4,128)(2,1)} %bitcast.3, ...), custom_call_target="tpu_custom_call" | custom-call | tf_op jit(solution)/shard_map/pallas_call | solution.py:342
  67.9 0.0 copy-start
  67.9 3.9 %copy.15 = bf16[1,384,4096]{2,1,0:T(8,128)(2,1)} copy(bf16[1,384,4096]{2,1,0:T(8,128)(2,1)} %get-tuple-element.4) | data formatting | bytes 6291456
  71.8 0.0 copy-done
  71.8 0.6 copy.16
Async XLA Ops:
  67.9 3.9 %copy-start = (bf16[4,4,1536]{2,1,0:T(4,128)(2,1)S(1)}, bf16[4,4,1536]{2,1,0:T(4,128)(2,1)}, u32[]{:S(2)}) copy-start(bf16[4,4,1536]{2,1,0:T(4,128)(2,1)} %get-tuple-element.5) | copy-start | bytes 147460
